TPU v7x, 256 devices: a whole 4x4x8 slice. The times are simulated.
256 devices in a mesh: lat: 16 (over y_lo, x, core), lon: 16 (over z, y_hi).
Axes of the slice: x: 4, y: 4 (y_hi: 2, y_lo: 2; y = y_hi * 2 + y_lo), z: 8, core: 2. Of those that a mesh axis runs over, the one named last changes fastest.
Arguments:
- fields: float32 [2, 192, 768, 192], P(None, 'lat', 'lon'), may hold values from -6 to 6
- cotangent: float32 [2, 192, 768, 192], P(None, 'lat', 'lon'), may hold values from -6 to 6
- norm_gain: float32 [192], replicated, may hold values from 0.1 to 1.9
- qkv_weight: float32 [192, 576], replicated, may hold values from -0.4375 to 0.4375
- out_weight: float32 [192, 192], replicated, may hold values from -0.4375 to 0.4375
- bias_table: float32 [32, 6, 3312], P('lat'), may hold values from -310 to 310, as said below
Outputs:
- branch: float32 [2, 192, 768, 192], P(None, 'lat', 'lon')
- grad_fields: float32 [2, 192, 768, 192], P(None, 'lat', 'lon')
- grad_gain: float32 [192], replicated
- grad_qkv: float32 [192, 576], replicated
- grad_out: float32 [192, 192], replicated
- grad_table: float32 [32, 6, 3312], P('lat')
Inputs may be any that keep to these rules, and one draw needn't show every extreme that they name: `bias_table`: entries of the bias tables.
All inputs are finite; a program needn't handle non-finite values.
Results may differ from a plain program's by a relative error of at most 0.0003.
Values sent between devices are 32-bit elements; how exact they have to be, the bound alone decides.
A program may use at most 128 MiB of HBM per device.

v0:
```python
import math
import jax
import jax.numpy as jnp
from jax import lax
from jax.experimental import pallas as pl
from jax.experimental.pallas import tpu as pltpu
from jax.sharding import PartitionSpec as P

WIN_LAT = 6
WIN_LON = 12
EPSILON = 1e-05
MASKED = -1000000000.0
HEADS = 6
HEAD = 32
D = 192
TOK = 144
WINDOWS = 8
OUTER = 12
SPAN = 23
F32 = jnp.float32
BF16 = jnp.bfloat16
NN = (((1,), (0,)), ((), ()))
NT = (((1,), (1,)), ((), ()))


def mm(a, b, dims=NN):
    return lax.dot_general(a, b, dims, preferred_element_type=F32)


def split(x):
    hi = x.astype(BF16)
    return hi, (x - hi.astype(F32)).astype(BF16)


def mm3(a, b, dims=NN):
    return mm(a[0], b[0], dims) + mm(a[0], b[1], dims) + mm(a[1], b[0], dims)


def selector(lo, length):
    row = lax.broadcasted_iota(jnp.int32, (length, TOK), 0)
    col = lax.broadcasted_iota(jnp.int32, (length, TOK), 1)
    picked = (col // WIN_LON) * SPAN + col % WIN_LON - lo + WIN_LON - 1
    return (row == picked).astype(F32).astype(BF16)


MESH = pl.DeviceIdType.MESH
LATS = 16
LONS = 16
CHIPS = 8


def remote(src, dst, send, recv, target):
    return pltpu.make_async_remote_copy(
        src_ref=src, dst_ref=dst, send_sem=send, recv_sem=recv, device_id=target, device_id_type=MESH)


def every(first, last):
    return pl.loop(first, last, unroll=True)


def main_kernel(
    f_ref, g_ref, gain_ref, wqkv_ref, wout_ref, table_ref,
    out_b, out_g, rows_b, rows_g, cols_b, cols_g, total, first_total, second_total,
    ext_f, ext_g,
    xs, ups, inv_s, s_hi, s_lo,
    kcat, vcat, q_hi, q_lo, do_hi, do_lo,
    qt, kt, vt, dot_, bias, dsacc, bias_raw,
    mix, dq, dk, dv, mix_t, sums_ref, chunks, first_part, second_part,
    half, recv_p, recv_a, first_recv, second_recv, tab_raw, o_s,
    local_sem, in_send, in_recv, halo_send, halo_recv, p_send, p_recv, a_send, a_recv,
    t_send, t_recv, b_send, b_recv, c_send, c_recv, d_send, d_recv, m_send, m_recv, e_send, e_recv,
):
    lat = lax.axis_index("lat")
    lon = lax.axis_index("lon")
    chip = lax.div(lat, 2)
    core = lax.rem(lat, 2)
    mate = chip * 2 + 1 - core
    up, down = lax.rem(lat + 1, LATS), lax.rem(lat + LATS - 1, LATS)
    right, left = lax.rem(lon + 1, LONS), lax.rem(lon + LONS - 1, LONS)
    local = []
    for i, (src, dst) in enumerate(((f_ref, ext_f), (g_ref, ext_g))):
        copy = pltpu.make_async_copy(
            src.at[:, pl.ds(3, 9)], dst.at[:, pl.ds(0, 9), pl.ds(0, 48)], local_sem.at[i])
        copy.start()
        local.append(copy)
    barrier = pltpu.get_barrier_semaphore()

    def greet(target):
        pl.semaphore_signal(barrier, inc=1, device_id=target, device_id_type=MESH)

    @every(1, LONS)
    def _(k):
        greet((lat, lax.rem(lon + k, LONS)))

    @every(1, LATS)
    def _(k):
        greet((lax.rem(lat + k, LATS), lon))

    greet((up, right))
    greet((down, left))
    pl.semaphore_wait(barrier, 32)
    halos_in = []
    for i, (src, dst) in enumerate(((f_ref, ext_f), (g_ref, ext_g))):
        pieces = (
            (src.at[:, pl.ds(3, 9), pl.ds(0, 8)], dst.at[:, pl.ds(0, 9), pl.ds(48, 8)], (lat, left)),
            (src.at[:, pl.ds(0, 3), pl.ds(0, 8)], dst.at[:, pl.ds(9, 3), pl.ds(48, 8)], (down, left)),
            (src.at[:, pl.ds(0, 3)], dst.at[:, pl.ds(9, 3), pl.ds(0, 48)], (down, lon)),
        )
        for j, (a, b, target) in enumerate(pieces):
            copy = remote(a, b, in_send.at[i * 3 + j], in_recv.at[i * 3 + j], target)
            copy.start()
            halos_in.append(copy)

    factor = HEAD ** (-0.5)
    gain = gain_ref[...]
    w = wqkv_ref[...]
    wq = w[:, :D] * factor
    wk = w[:, D:2 * D]
    wv = w[:, 2 * D:]

    def replicated(m):
        parts = []
        for h in range(HEADS):
            parts += [m[:, h * HEAD:(h + 1) * HEAD]] * 4
        return jnp.concatenate(parts, axis=1)

    wkr = split(replicated(wk))
    wvr = split(replicated(wv))
    wqs = split(wq)
    wt = split(jnp.concatenate([wq.T, wk.T, wv.T], axis=0))
    wo = split(wout_ref[...])
    wks = split(wk)
    wvs = split(wv)
    wqp = split(w[:, :D])

    for a in range(2):
        for h in range(HEADS):
            for i in range(OUTER):
                at = (a * HEADS + h) * OUTER + i
                tab_raw[at:at + 1, :] = table_ref[h, a:a + 1, i * OUTER * SPAN:(i + 1) * OUTER * SPAN]
    t0 = tab_raw[...]
    t_hi = t0.astype(BF16)
    rest = t0 - t_hi.astype(F32)
    t_mid = rest.astype(BF16)
    t_lo = (rest - t_mid.astype(F32)).astype(BF16)
    for lo in range(WIN_LON):
        sel = selector(lo, OUTER * SPAN)
        bias_raw[:, lo, :] = mm(t_hi, sel) + mm(t_mid, sel) + mm(t_lo, sel)
    row = lax.broadcasted_iota(jnp.int32, (TOK, TOK), 0)
    col = lax.broadcasted_iota(jnp.int32, (TOK, TOK), 1)
    half_r = (row // WIN_LON) % WIN_LAT < WIN_LAT // 2
    half_c = (col // WIN_LON) % WIN_LAT < WIN_LAT // 2
    apart = half_r != half_c
    for a in range(2):
        on_seam = lat * 2 + a == 31
        cut = jnp.logical_and(apart, on_seam)
        for h in range(HEADS):
            g = a * HEADS + h
            b = bias_raw[g * OUTER:(g + 1) * OUTER].reshape(TOK, TOK)
            bias[g] = jnp.where(cut, MASKED, b.T)
            dsacc[g] = jnp.zeros((TOK, TOK), F32)

    def front(first_window, last_window):
        for wi in range(first_window, last_window):
            a, b = divmod(wi, 4)
            for l in range(2):
                for r in range(WIN_LAT):
                    at = wi * TOK + (l * WIN_LAT + r) * WIN_LON
                    c0 = 6 + WIN_LON * b
                    xs[at:at + WIN_LON, :] = ext_f[l, a * WIN_LAT + r, c0:c0 + WIN_LON, :]
                    ups[at:at + WIN_LON, :] = ext_g[l, a * WIN_LAT + r, c0:c0 + WIN_LON, :]

        @pl.loop(first_window, last_window)
        def _(wi):
            rows = pl.ds(pl.multiple_of(wi * TOK, TOK), TOK)
            x = xs[rows, :]
            c = x - jnp.mean(x, axis=-1, keepdims=True)
            inv = lax.rsqrt(jnp.mean(c * c, axis=-1, keepdims=True) + EPSILON)
            n = c * inv
            xs[rows, :] = n
            inv_s[rows, :] = jnp.broadcast_to(inv, (TOK, 128))
            s = split(n * gain)
            s_hi[rows, :] = s[0]
            s_lo[rows, :] = s[1]
            pt = mm3(wt, s, NT)
            for i, ref in enumerate((qt, kt, vt)):
                ph, pll = split(pt[i * D:(i + 1) * D])
                for h in range(HEADS):
                    a_, b_ = ph[h * HEAD:(h + 1) * HEAD], pll[h * HEAD:(h + 1) * HEAD]
                    if ref is qt:
                        ref[wi, h] = jnp.concatenate([a_, b_, a_, b_], axis=0)
                    else:
                        ref[wi, h] = jnp.concatenate([a_, b_], axis=0)
            u = split(ups[rows, :])
            dt = split(mm3(wo, u, NT))
            for h in range(HEADS):
                a_, b_ = dt[0][h * HEAD:(h + 1) * HEAD], dt[1][h * HEAD:(h + 1) * HEAD]
                dot_[wi, h] = jnp.concatenate([a_, b_, a_, b_], axis=0)

        size = (last_window - first_window) * TOK
        rows = slice(first_window * TOK, last_window * TOK)
        first_half = lax.broadcasted_iota(jnp.int32, (size, 256), 1) % 128 < 64
        left_side = (s_hi[rows, :], s_lo[rows, :])
        for j in range(3):
            cols = slice(j * 256, (j + 1) * 256)
            for wr, ref in ((wkr, kcat), (wvr, vcat)):
                ph, pll = split(mm3(left_side, (wr[0][:, cols], wr[1][:, cols])))
                ref[rows, cols] = jnp.where(first_half, ph, pll)
        qh, ql = split(mm3(left_side, wqs))
        q_hi[rows, :] = qh
        q_lo[rows, :] = ql
        dh, dl = split(mm3(split(ups[rows, :]), wo, NT))
        do_hi[rows, :] = dh
        do_lo[rows, :] = dl

    for copy in local:
        copy.wait()
    front(0, 3)
    class LonSum:
        def __init__(self, src, recv, out, s1, r1, s2, r2):
            self.refs = src, recv, out, s1, r1, s2, r2

        def scatter_copy(self, k):
            src, recv, out, s1, r1, s2, r2 = self.refs
            peer = lax.rem(lon + k, LONS)
            return remote(src.at[peer], recv.at[k - 1], s1.at[k - 1], r1.at[k - 1], (lat, peer))

        def gather_copy(self, k, owner, peer):
            src, recv, out, s1, r1, s2, r2 = self.refs
            return remote(out.at[owner], out.at[owner], s2.at[k - 1], r2.at[k - 1], (lat, peer))

        def start(self):
            @every(1, LONS)
            def _(k):
                self.scatter_copy(k).start()

        def middle(self):
            src, recv, out = self.refs[:3]

            @every(1, LONS)
            def _(k):
                self.scatter_copy(k).wait()

            own = src[lon]
            for k in range(LONS - 1):
                own += recv[k]
            out[lon] = own

            @every(1, LONS)
            def _(k):
                self.gather_copy(k, lon, lax.rem(lon + k, LONS)).start()

        def end(self):
            @every(1, LONS)
            def _(k):
                self.gather_copy(k, lon, lax.rem(lon + k, LONS)).wait_send()
                owner = lax.rem(lon + LONS - k, LONS)
                self.gather_copy(k, owner, owner).wait_recv()

    first = LonSum(first_part, first_recv, first_total, t_send, t_recv, e_send, e_recv)
    second = LonSum(second_part, second_recv, second_total, b_send, b_recv, c_send, c_recv)

    def place(ref, t, value):
        q, s = divmod(t, 2)
        ref[q, s * 8:s * 8 + 8, :] = value

    def table_gradient(a, ref):
        for g in range(a * HEADS, (a + 1) * HEADS):
            bias_raw[g * OUTER:(g + 1) * OUTER] = dsacc[g].T.reshape(OUTER, WIN_LON, TOK)
        acc = jnp.zeros((72, 384), F32)
        for lo in range(WIN_LON):
            sel = selector(lo, 384)
            d_hi, d_lo = split(bias_raw[a * 72:(a + 1) * 72, lo, :])
            acc += mm(d_hi, sel, NT) + mm(d_lo, sel, NT)
        for i in range(9):
            for j in range(2):
                place(ref, i * 2 + j, acc[i * 8:i * 8 + 8, j * 128:(j + 1) * 128])
        for p, members in enumerate((range(6), range(6, 9))):
            packed = jnp.zeros((8, 128), F32)
            for i in members:
                tail = acc[i * 8:i * 8 + 8, 256:]
                turn = 20 * (i % 6)
                packed += tail if turn == 0 else pltpu.roll(tail, turn, 1)
            place(ref, 18 + p, packed)

    def scatter(wi, src, out):
        a, b = divmod(wi, 4)
        for l in range(2):
            for r in range(WIN_LAT):
                at = wi * TOK + (l * WIN_LAT + r) * WIN_LON
                c0 = 6 + WIN_LON * b
                out[l, a * WIN_LAT + r, c0:c0 + WIN_LON, :] = src[at:at + WIN_LON, :]

    def halo_copy(i, j, src, dst, target):
        return remote(src, dst, halo_send.at[i * 4 + j], halo_recv.at[i * 4 + j], target)

    def halo_first(i, out, cols):
        return halo_copy(i, 0, out.at[:, pl.ds(0, 6), pl.ds(48, 8)], cols.at[:, pl.ds(3, 6)], (lat, right))

    def halo_second(i, out, cols):
        return halo_copy(i, 1, out.at[:, pl.ds(6, 3), pl.ds(48, 8)], cols.at[:, pl.ds(9, 3)], (lat, right))

    def halo_corner(i, out, cols):
        return halo_copy(i, 2, out.at[:, pl.ds(9, 3), pl.ds(48, 8)], cols.at[:, pl.ds(0, 3)], (up, right))

    def halo_rows(i, out, edge):
        return halo_copy(i, 3, out.at[:, pl.ds(9, 3), pl.ds(0, 48)], edge, (up, lon))

    def branch_of(wi):
        rows = pl.ds(pl.multiple_of(wi * TOK, TOK), TOK)
        o_s[rows, :] = mm3(split(mix[wi].T), wo)

    for i in range(10, 16):
        first_part[i] = jnp.zeros((16, 128), F32)
    second_part[14, 8:16, :] = jnp.zeros((8, 128), F32)
    second_part[15] = jnp.zeros((16, 128), F32)

    head_of = lax.broadcasted_iota(jnp.int32, (TOK, D), 1) // HEAD

    @pl.loop(0, WINDOWS)
    def _(wi):
        @pl.when(wi == 3)
        def _():
            for copy in halos_in:
                copy.wait()
            front(3, WINDOWS)

        @pl.when(wi == 4)
        def _():
            table_gradient(0, first_part)
            first.start()
            pl.loop(0, 4)(branch_of)
            for w in range(4):
                scatter(w, o_s, out_b)
            halo_first(0, out_b, cols_b).start()

        @pl.when(wi == 7)
        def _():
            first.middle()

        rows = pl.ds(pl.multiple_of(wi * TOK, TOK), TOK)
        base = lax.div(wi, 4) * HEADS
        dv_acc = jnp.zeros((TOK, D), F32)
        dk_acc = jnp.zeros((TOK, D), F32)
        zero = jnp.zeros((TOK, D), BF16)
        for h in range(HEADS):
            blk = slice(h * 128, (h + 1) * 128)
            st = mm(kcat[rows, blk], qt[wi, h]) + bias[base + h]
            e = jnp.exp(st - jnp.max(st, axis=0, keepdims=True))
            p = e * (1.0 / jnp.sum(e, axis=0, keepdims=True))
            p_hi, p_lo = split(p)
            dp = mm(vcat[rows, blk], dot_[wi, h])
            ds = p * (dp - jnp.sum(p * dp, axis=0, keepdims=True))
            dsacc[base + h] += ds
            ds_hi, ds_lo = split(ds)
            v2 = vt[wi, h]
            m2 = mm(v2, p_hi)
            m = m2[:HEAD] + m2[HEAD:] + mm(v2[:HEAD], p_lo)
            mix_t[h * HEAD:(h + 1) * HEAD, :] = m
            k2 = kt[wi, h]
            g2 = mm(k2, ds_hi)
            g = g2[:HEAD] + g2[HEAD:] + mm(k2[:HEAD], ds_lo)
            dq[wi, h * HEAD:(h + 1) * HEAD, :] = g * factor
            mine = head_of == h
            o_hi = jnp.where(mine, do_hi[rows, :], zero)
            o_lo = jnp.where(mine, do_lo[rows, :], zero)
            dv_acc += mm(p_hi, o_hi) + mm(p_hi, o_lo) + mm(p_lo, o_hi)
            c_hi = jnp.where(mine, q_hi[rows, :], zero)
            c_lo = jnp.where(mine, q_lo[rows, :], zero)
            dk_acc += mm(ds_hi, c_hi) + mm(ds_hi, c_lo) + mm(ds_lo, c_hi)
        dv[rows, :] = dv_acc
        dk[rows, :] = dk_acc
        mix[wi] = mix_t[...]

    pl.loop(4, WINDOWS)(branch_of)
    for wi in range(4, WINDOWS):
        scatter(wi, o_s, out_b)
    halo_second(0, out_b, cols_b).start()
    halo_corner(0, out_b, cols_b).start()
    halo_rows(0, out_b, rows_b).start()

    sums_ref[...] = jnp.zeros_like(sums_ref)

    @pl.loop(0, WINDOWS)
    def _(wi):
        rows = pl.ds(pl.multiple_of(wi * TOK, TOK), TOK)
        nt = split(xs[rows, :].T)
        sums_ref[:, 3 * D:] += mm3(split(mix[wi]), split(ups[rows, :]))
        sums_ref[:, :D] += mm3(nt, split(dq[wi].T))
        sums_ref[:, D:2 * D] += mm3(nt, split(dk[rows, :]))
        sums_ref[:, 2 * D:3 * D] += mm3(nt, split(dv[rows, :]))

    for i in range(24):
        for j in range(6):
            q, s = divmod(i * 6 + j, 9)
            chunks[q // 2, q % 2, s * 8:s * 8 + 8, :] = sums_ref[i * 8:i * 8 + 8, j * 128:(j + 1) * 128]
    pair = remote(chunks.at[:, 1 - core], recv_p, p_send, p_recv, (mate, lon))
    pair.start()

    table_gradient(1, second_part)
    pair.wait()
    half[...] = chunks[:, core] + recv_p[...]

    def stage_a(k):
        peer = lax.rem(chip + k, CHIPS)
        return remote(half.at[peer], recv_a.at[k - 1], a_send.at[k - 1], a_recv.at[k - 1], (peer * 2 + core, lon))

    @every(1, CHIPS)
    def _(k):
        stage_a(k).start()

    def rest_of(wi):
        rows = pl.ds(pl.multiple_of(wi * TOK, TOK), TOK)
        n = xs[rows, :]
        grad_scaled = (
            mm3(split(dq[wi].T), wqp, NT) + mm3(split(dk[rows, :]), wks, NT) + mm3(split(dv[rows, :]), wvs, NT)
        )
        g = grad_scaled * gain
        o_s[rows, :] = inv_s[rows, :][:, :1] * (
            g - jnp.mean(g, axis=-1, keepdims=True)
            - n * jnp.mean(g * n, axis=-1, keepdims=True)
        )

    pl.loop(4, WINDOWS)(rest_of)
    for wi in range(4, WINDOWS):
        scatter(wi, o_s, out_g)

    @every(1, CHIPS)
    def _(k):
        stage_a(k).wait()

    own = half[chip]
    for k in range(CHIPS - 1):
        own += recv_a[k]
    for t in range(9):
        place(second_part, 20 + t, own[t * 8:t * 8 + 8])
    second.start()
    halo_rows(1, out_g, rows_g).start()

    pl.loop(0, 4)(rest_of)
    for wi in range(4):
        scatter(wi, o_s, out_g)

    second.middle()
    halo_first(1, out_g, cols_g).start()
    halo_second(1, out_g, cols_g).start()
    halo_corner(1, out_g, cols_g).start()
    first.end()
    second.end()
    total[chip, core] = second_total[10:15]

    def stage_d(k, owner, peer):
        here = total.at[owner, core]
        return remote(here, here, d_send.at[k - 1], d_recv.at[k - 1], (peer * 2 + core, lon))

    @every(1, CHIPS)
    def _(k):
        stage_d(k, chip, lax.rem(chip + k, CHIPS)).start()

    @every(1, CHIPS)
    def _(k):
        owner = lax.rem(chip + CHIPS - k, CHIPS)
        stage_d(k, owner, owner).wait_recv()

    ours = total.at[:, core]
    swap = remote(ours, ours, m_send, m_recv, (mate, lon))
    swap.start()

    @every(1, CHIPS)
    def _(k):
        stage_d(k, chip, lax.rem(chip + k, CHIPS)).wait_send()

    for i, (out, edge, cols) in enumerate(((out_b, rows_b, cols_b), (out_g, rows_g, cols_g))):
        halo_rows(i, out, edge).wait()
        halo_first(i, out, cols).wait()
        halo_second(i, out, cols).wait()
        halo_corner(i, out, cols).wait()

    swap.wait_send()
    theirs = total.at[:, 1 - core]
    remote(theirs, theirs, m_send, m_recv, (mate, lon)).wait_recv()


def main(fields, cotangent, gain, wqkv, wout, table):
    vm = pl.BlockSpec(memory_space=pltpu.VMEM)
    anywhere = pl.BlockSpec(memory_space=pl.ANY)
    rows = WINDOWS * TOK
    DMA = pltpu.SemaphoreType.DMA
    scratch = [
        pltpu.VMEM((2, 12, 56, D), F32), pltpu.VMEM((2, 12, 56, D), F32),
        pltpu.VMEM((rows, D), F32), pltpu.VMEM((rows, D), F32), pltpu.VMEM((rows, 128), F32),
        pltpu.VMEM((rows, D), BF16), pltpu.VMEM((rows, D), BF16),
        pltpu.VMEM((rows, 768), BF16), pltpu.VMEM((rows, 768), BF16),
        pltpu.VMEM((rows, D), BF16), pltpu.VMEM((rows, D), BF16),
        pltpu.VMEM((rows, D), BF16), pltpu.VMEM((rows, D), BF16),
        pltpu.VMEM((WINDOWS, HEADS, 128, TOK), BF16),
        pltpu.VMEM((WINDOWS, HEADS, 64, TOK), BF16),
        pltpu.VMEM((WINDOWS, HEADS, 64, TOK), BF16),
        pltpu.VMEM((WINDOWS, HEADS, 128, TOK), BF16),
        pltpu.VMEM((2 * HEADS, TOK, TOK), F32),
        pltpu.VMEM((2 * HEADS, TOK, TOK), F32),
        pltpu.VMEM((TOK, WIN_LON, TOK), F32),
        pltpu.VMEM((WINDOWS, D, TOK), F32), pltpu.VMEM((WINDOWS, D, TOK), F32),
        pltpu.VMEM((rows, D), F32), pltpu.VMEM((rows, D), F32),
        pltpu.VMEM((D, TOK), F32),
        pltpu.VMEM((D, 4 * D), F32),
        pltpu.VMEM((8, 2, 72, 128), F32), pltpu.VMEM((16, 16, 128), F32), pltpu.VMEM((16, 16, 128), F32),
        pltpu.VMEM((8, 72, 128), F32), pltpu.VMEM((8, 72, 128), F32), pltpu.VMEM((7, 72, 128), F32),
        pltpu.VMEM((15, 16, 128), F32), pltpu.VMEM((15, 16, 128), F32),
        pltpu.VMEM((TOK, OUTER * SPAN), F32), pltpu.VMEM((rows, D), F32),
        DMA((2,)), DMA((6,)), DMA((6,)), DMA((8,)), DMA((8,)), DMA, DMA, DMA((7,)), DMA((7,)),
        DMA((15,)), DMA((15,)), DMA((15,)), DMA((15,)), DMA((15,)), DMA((15,)),
        DMA((7,)), DMA((7,)), DMA, DMA, DMA((15,)), DMA((15,)),
    ]
    whole = jax.ShapeDtypeStruct((2, 12, 56, D), F32)
    edge = jax.ShapeDtypeStruct((2, 3, 48, D), F32)
    side = jax.ShapeDtypeStruct((2, 12, 8, D), F32)
    return pl.pallas_call(
        main_kernel,
        out_shape=[
            whole, whole, edge, edge, side, side,
            jax.ShapeDtypeStruct((8, 2, 5, 16, 128), F32),
            jax.ShapeDtypeStruct((16, 16, 128), F32), jax.ShapeDtypeStruct((16, 16, 128), F32),
        ],
        in_specs=[anywhere] * 2 + [vm] * 4,
        out_specs=[vm] * 9,
        scratch_shapes=scratch,
        compiler_params=pltpu.CompilerParams(
            collective_id=0, has_side_effects=True, vmem_limit_bytes=60 * 1024 * 1024),
    )(fields, cotangent, gain, wqkv, wout, table)


def finish_kernel(
    ext_b, ext_g, rows_b, rows_g, cols_b, cols_g, total, first_total, second_total, wqkv_ref, gain_ref,
    branch, grads, gain_out, qkv_out, out_out, table_out, full, flat,
):
    for ext, rows, cols, out in ((ext_b, rows_b, cols_b, branch), (ext_g, rows_g, cols_g, grads)):
        out[:, 0:3] = rows[...]
        out[:, 3:12] = ext[:, 0:9, 0:48, :]
        there = lax.broadcasted_iota(jnp.int32, (2, 12, 8, D), 2) < 6
        out[:, :, 0:8, :] = jnp.where(there, cols[...], out[:, :, 0:8, :])
    scale = 1.0 / math.sqrt(LATS * LONS * WINDOWS * TOK)
    for i in range(24):
        for j in range(6):
            q, s = divmod(i * 6 + j, 9)
            full[i * 8:i * 8 + 8, j * 128:(j + 1) * 128] = total[q // 2, q % 2, s // 2, s % 2 * 8:s % 2 * 8 + 8, :] * scale
    raw = full[:, :3 * D]
    summed = jnp.sum(raw * wqkv_ref[...], axis=1, keepdims=True)
    gain_out[...] = jnp.broadcast_to(summed, (D, 128)).T[:1]
    qkv_out[...] = raw * jnp.broadcast_to(gain_ref[...], (8, D)).T[:, :1]
    out_out[...] = full[:, 3 * D:]
    def tile(ref, t):
        q, s = divmod(t, 2)
        return ref[q, s * 8:s * 8 + 8, :]

    for a, ref in enumerate((first_total, second_total)):
        for i in range(9):
            at = a * 72 + i * 8
            for j in range(2):
                flat[at:at + 8, j * 128:(j + 1) * 128] = tile(ref, i * 2 + j)
            packed = tile(ref, 18 + i // 6)
            turn = 20 * (i % 6)
            flat[at:at + 8, 256:384] = packed if turn == 0 else pltpu.roll(packed, 128 - turn, 1)
    for a in range(2):
        for h in range(HEADS):
            for i in range(OUTER):
                at = (a * HEADS + h) * OUTER + i
                table_out[h, a:a + 1, i * OUTER * SPAN:(i + 1) * OUTER * SPAN] = flat[at:at + 1, :OUTER * SPAN]


def finish(ext_b, ext_g, rows_b, rows_g, cols_b, cols_g, total, first_total, second_total, wqkv, gain):
    vm = pl.BlockSpec(memory_space=pltpu.VMEM)
    whole = jax.ShapeDtypeStruct((2, 12, 48, D), F32)
    return pl.pallas_call(
        finish_kernel,
        out_shape=[
            whole, whole, jax.ShapeDtypeStruct((1, D), F32), jax.ShapeDtypeStruct((D, 3 * D), F32),
            jax.ShapeDtypeStruct((D, D), F32), jax.ShapeDtypeStruct((HEADS, 2, OUTER * OUTER * SPAN), F32),
        ],
        in_specs=[vm] * 11,
        out_specs=[vm] * 6,
        scratch_shapes=[pltpu.VMEM((D, 4 * D), F32), pltpu.VMEM((TOK, 384), F32)],
        compiler_params=pltpu.CompilerParams(vmem_limit_bytes=60 * 1024 * 1024),
    )(ext_b, ext_g, rows_b, rows_g, cols_b, cols_g, total, first_total, second_total, wqkv, gain)


def on_device(fields, cotangent, norm_gain, qkv_weight, out_weight, bias_table):
    table = jnp.transpose(bias_table, (1, 0, 2))
    win_b, win_g, rows_b, rows_g, cols_b, cols_g, total, first_total, second_total = main(
        fields, cotangent, norm_gain.reshape(1, D), qkv_weight, out_weight, table)
    branch, grad_fields, gain, qkv, out, gtable = finish(
        win_b, win_g, rows_b, rows_g, cols_b, cols_g, total, first_total, second_total, qkv_weight, norm_gain.reshape(1, D))
    return branch, grad_fields, gain.reshape(D), qkv, out, jnp.transpose(gtable, (1, 0, 2))


def solution(mesh):
    cells = P(None, "lat", "lon", None)
    rows = P("lat", None, None)
    return jax.shard_map(
        on_device,
        mesh=mesh,
        in_specs=(cells, cells, P(), P(), P(), rows),
        out_specs=(cells, cells, P(), P(), P(), rows),
        check_vma=False,
    )
```

profile of v0, /device:TPU:1, one launch (start us, length us, event | category | flops | bytes accessed | tf_op | source)
XLA Modules:
  0.0 96.9 jit_solution(13681927842142739383)
XLA Ops:
  0.6 91.6 %shard_map.109 = (f32[2,12,56,192]{3,2,1,0:T(8,128)}, f32[2,12,56,192]{3,2,1,0:T(8,128)}, f32[2,3,48,192]{3,2,1,0:T(8,128)}, f32[2,3,48,192]{3,2,1,0:T(8,128)}, ...) custom-call(f32[2,12,48,192]{3,2,1,0:T(8,128)} %f_ref.1, ...), custom_call_target="tpu_custom_call" | custom-call | tf_op jit(solution)/shard_map/pallas_call | solution.py:518
  92.3 4.6 %shard_map.110 = (f32[2,12,48,192]{3,2,1,0:T(8,128)}, f32[2,12,48,192]{3,2,1,0:T(8,128)}, f32[1,192]{1,0:T(1,128)}, f32[192,576]{1,0:T(8,128)}, f32[192,192]{1,0:T(8,128)}, /*index=5*/f32[6,2,3312]{2,1,0:T(2,128)}) custom-call(f32[2,12,56,192]{3,2,1,0:T(8,128)} %get-tuple-element.21.ext_b, f32[2,12,56,192]{3,2,1,0:T(8,128)} %get-tuple-element.22.ext_g, ...), custom_call_target="tpu_custom_call" | custom-call | tf_op jit(solution)/shard_map/pallas_call | solution.py:574
where the time goes:
time: 97 us; the launch traced here: 96.9 us
  Pallas kernels  96.2 us (99%)
    pallas_call x1, Pallas kernels, main(): pl.pallas_call(main_kernel, out_shape=[whole, whole, edge, edge, side, si...  91.6 us
    pallas_call x1, Pallas kernels, finish(): pl.pallas_call(finish_kernel, out_shape=[whole, whole, jax.ShapeDtypeStru...  4.6 us

commit v1 on v0

--- a/solution.py
+++ b/solution.py
@@ -60,21 +60,24 @@
 
 def main_kernel(
     f_ref, g_ref, gain_ref, wqkv_ref, wout_ref, table_ref,
-    out_b, out_g, rows_b, rows_g, cols_b, cols_g, total, first_total, second_total,
-    ext_f, ext_g,
+    own_b, own_g, rows_b, rows_g, cols_b, cols_g, total, first_total, second_total,
+    ext_f, ext_g, out_b, out_g,
     xs, ups, inv_s, s_hi, s_lo,
     kcat, vcat, q_hi, q_lo, do_hi, do_lo,
     qt, kt, vt, dot_, bias, dsacc, bias_raw,
     mix, dq, dk, dv, mix_t, sums_ref, chunks, first_part, second_part,
-    half, recv_p, recv_a, first_recv, second_recv, tab_raw, o_s,
-    local_sem, in_send, in_recv, halo_send, halo_recv, p_send, p_recv, a_send, a_recv,
-    t_send, t_recv, b_send, b_recv, c_send, c_recv, d_send, d_recv, m_send, m_recv, e_send, e_recv,
+    half, recv_p, recv_a, z_all, first_recv, second_recv, tab_raw, o_s,
+    local_sem, own_sem, in_send, in_recv, halo_send, halo_recv, p_send, p_recv, a_send, a_recv,
+    t_send, t_recv, b_send, b_recv, c_send, c_recv, d_send, d_recv, m_send, m_recv, e_send, e_recv, z_send, z_recv,
 ):
     lat = lax.axis_index("lat")
     lon = lax.axis_index("lon")
     chip = lax.div(lat, 2)
     core = lax.rem(lat, 2)
     mate = chip * 2 + 1 - core
+    y_hi = lax.rem(lon, 2)
+    z = lax.div(lon, 2)
+    plane = chip * 2 + y_hi
     up, down = lax.rem(lat + 1, LATS), lax.rem(lat + LATS - 1, LATS)
     right, left = lax.rem(lon + 1, LONS), lax.rem(lon + LONS - 1, LONS)
     local = []
@@ -92,13 +95,17 @@
     def _(k):
         greet((lat, lax.rem(lon + k, LONS)))
 
-    @every(1, LATS)
-    def _(k):
-        greet((lax.rem(lat + k, LATS), lon))
-
+    @every(1, CHIPS)
+    def _(k):
+        other = lax.rem(chip + k, CHIPS) * 2 + core
+        greet((other, z * 2))
+        greet((other, z * 2 + 1))
+
+    greet((up, lon))
+    greet((down, lon))
     greet((up, right))
     greet((down, left))
-    pl.semaphore_wait(barrier, 32)
+    pl.semaphore_wait(barrier, 33)
     halos_in = []
     for i, (src, dst) in enumerate(((f_ref, ext_f), (g_ref, ext_g))):
         pieces = (
@@ -312,8 +319,10 @@
 
     for i in range(10, 16):
         first_part[i] = jnp.zeros((16, 128), F32)
-    second_part[14, 8:16, :] = jnp.zeros((8, 128), F32)
-    second_part[15] = jnp.zeros((16, 128), F32)
+        second_part[i] = jnp.zeros((16, 128), F32)
+    chunks[14, 0, 32:40, :] = jnp.zeros((8, 128), F32)
+    chunks[14, 1] = jnp.zeros((40, 128), F32)
+    chunks[15] = jnp.zeros((2, 40, 128), F32)
 
     head_of = lax.broadcasted_iota(jnp.int32, (TOK, D), 1) // HEAD
 
@@ -372,13 +381,6 @@
         dk[rows, :] = dk_acc
         mix[wi] = mix_t[...]
 
-    pl.loop(4, WINDOWS)(branch_of)
-    for wi in range(4, WINDOWS):
-        scatter(wi, o_s, out_b)
-    halo_second(0, out_b, cols_b).start()
-    halo_corner(0, out_b, cols_b).start()
-    halo_rows(0, out_b, rows_b).start()
-
     sums_ref[...] = jnp.zeros_like(sums_ref)
 
     @pl.loop(0, WINDOWS)
@@ -392,22 +394,35 @@
 
     for i in range(24):
         for j in range(6):
-            q, s = divmod(i * 6 + j, 9)
+            q, s = divmod(i * 6 + j, 5)
             chunks[q // 2, q % 2, s * 8:s * 8 + 8, :] = sums_ref[i * 8:i * 8 + 8, j * 128:(j + 1) * 128]
     pair = remote(chunks.at[:, 1 - core], recv_p, p_send, p_recv, (mate, lon))
     pair.start()
-
     table_gradient(1, second_part)
     pair.wait()
     half[...] = chunks[:, core] + recv_p[...]
 
+    def plane_device(q):
+        return (lax.div(q, 2) * 2 + core, z * 2 + lax.rem(q, 2))
+
     def stage_a(k):
-        peer = lax.rem(chip + k, CHIPS)
-        return remote(half.at[peer], recv_a.at[k - 1], a_send.at[k - 1], a_recv.at[k - 1], (peer * 2 + core, lon))
-
-    @every(1, CHIPS)
+        peer = lax.rem(plane + k, 16)
+        return remote(half.at[peer], recv_a.at[k - 1], a_send.at[k - 1], a_recv.at[k - 1], plane_device(peer))
+
+    @every(1, 16)
     def _(k):
         stage_a(k).start()
+
+    second.start()
+
+    pl.loop(4, WINDOWS)(branch_of)
+    for wi in range(4, WINDOWS):
+        scatter(wi, o_s, out_b)
+
+    def own_copy(i, out, own):
+        return pltpu.make_async_copy(out.at[:, pl.ds(0, 9), pl.ds(0, 48)], own, own_sem.at[i])
+
+    own_copy(0, out_b, own_b).start()
 
     def rest_of(wi):
         rows = pl.ds(pl.multiple_of(wi * TOK, TOK), TOK)
@@ -425,51 +440,77 @@
     for wi in range(4, WINDOWS):
         scatter(wi, o_s, out_g)
 
-    @every(1, CHIPS)
+    @every(1, 16)
     def _(k):
         stage_a(k).wait()
 
-    own = half[chip]
-    for k in range(CHIPS - 1):
+    own = half[plane]
+    for k in range(15):
         own += recv_a[k]
-    for t in range(9):
-        place(second_part, 20 + t, own[t * 8:t * 8 + 8])
-    second.start()
+    z_all[z] = own
+
+    def stage_z(k, owner, peer):
+        here = z_all.at[owner]
+        return remote(here, here, z_send.at[k - 1], z_recv.at[k - 1], (lat, peer * 2 + y_hi))
+
+    @every(1, 8)
+    def _(k):
+        stage_z(k, z, lax.rem(z + k, 8)).start()
+
+    halo_second(0, out_b, cols_b).start()
+    halo_corner(0, out_b, cols_b).start()
+    halo_rows(0, out_b, rows_b).start()
     halo_rows(1, out_g, rows_g).start()
+    second.middle()
 
     pl.loop(0, 4)(rest_of)
     for wi in range(4):
         scatter(wi, o_s, out_g)
-
-    second.middle()
+    own_copy(1, out_g, own_g).start()
+
+    @every(1, 8)
+    def _(k):
+        owner = lax.rem(z + 8 - k, 8)
+        stage_z(k, owner, owner).wait_recv()
+
+    whole = z_all[0]
+    for k in range(1, 8):
+        whole += z_all[k]
+    total[plane, core] = whole
+
+    def stage_d(k, owner, peer):
+        here = total.at[owner, core]
+        return remote(here, here, d_send.at[k - 1], d_recv.at[k - 1], plane_device(peer))
+
+    @every(1, 16)
+    def _(k):
+        stage_d(k, plane, lax.rem(plane + k, 16)).start()
+
     halo_first(1, out_g, cols_g).start()
     halo_second(1, out_g, cols_g).start()
     halo_corner(1, out_g, cols_g).start()
-    first.end()
-    second.end()
-    total[chip, core] = second_total[10:15]
-
-    def stage_d(k, owner, peer):
-        here = total.at[owner, core]
-        return remote(here, here, d_send.at[k - 1], d_recv.at[k - 1], (peer * 2 + core, lon))
-
-    @every(1, CHIPS)
-    def _(k):
-        stage_d(k, chip, lax.rem(chip + k, CHIPS)).start()
-
-    @every(1, CHIPS)
-    def _(k):
-        owner = lax.rem(chip + CHIPS - k, CHIPS)
+
+    @every(1, 8)
+    def _(k):
+        stage_z(k, z, lax.rem(z + k, 8)).wait_send()
+
+    @every(1, 16)
+    def _(k):
+        owner = lax.rem(plane + 16 - k, 16)
         stage_d(k, owner, owner).wait_recv()
 
     ours = total.at[:, core]
     swap = remote(ours, ours, m_send, m_recv, (mate, lon))
     swap.start()
 
-    @every(1, CHIPS)
-    def _(k):
-        stage_d(k, chip, lax.rem(chip + k, CHIPS)).wait_send()
-
+    @every(1, 16)
+    def _(k):
+        stage_d(k, plane, lax.rem(plane + k, 16)).wait_send()
+
+    first.end()
+    second.end()
+    own_copy(0, out_b, own_b).wait()
+    own_copy(1, out_g, own_g).wait()
     for i, (out, edge, cols) in enumerate(((out_b, rows_b, cols_b), (out_g, rows_g, cols_g))):
         halo_rows(i, out, edge).wait()
         halo_first(i, out, cols).wait()
@@ -487,6 +528,7 @@
     rows = WINDOWS * TOK
     DMA = pltpu.SemaphoreType.DMA
     scratch = [
+        pltpu.VMEM((2, 12, 56, D), F32), pltpu.VMEM((2, 12, 56, D), F32),
         pltpu.VMEM((2, 12, 56, D), F32), pltpu.VMEM((2, 12, 56, D), F32),
         pltpu.VMEM((rows, D), F32), pltpu.VMEM((rows, D), F32), pltpu.VMEM((rows, 128), F32),
         pltpu.VMEM((rows, D), BF16), pltpu.VMEM((rows, D), BF16),
@@ -504,26 +546,27 @@
         pltpu.VMEM((rows, D), F32), pltpu.VMEM((rows, D), F32),
         pltpu.VMEM((D, TOK), F32),
         pltpu.VMEM((D, 4 * D), F32),
-        pltpu.VMEM((8, 2, 72, 128), F32), pltpu.VMEM((16, 16, 128), F32), pltpu.VMEM((16, 16, 128), F32),
-        pltpu.VMEM((8, 72, 128), F32), pltpu.VMEM((8, 72, 128), F32), pltpu.VMEM((7, 72, 128), F32),
+        pltpu.VMEM((16, 2, 40, 128), F32), pltpu.VMEM((16, 16, 128), F32), pltpu.VMEM((16, 16, 128), F32),
+        pltpu.VMEM((16, 40, 128), F32), pltpu.VMEM((16, 40, 128), F32), pltpu.VMEM((15, 40, 128), F32),
+        pltpu.VMEM((8, 40, 128), F32),
         pltpu.VMEM((15, 16, 128), F32), pltpu.VMEM((15, 16, 128), F32),
         pltpu.VMEM((TOK, OUTER * SPAN), F32), pltpu.VMEM((rows, D), F32),
-        DMA((2,)), DMA((6,)), DMA((6,)), DMA((8,)), DMA((8,)), DMA, DMA, DMA((7,)), DMA((7,)),
+        DMA((2,)), DMA((2,)), DMA((6,)), DMA((6,)), DMA((8,)), DMA((8,)), DMA, DMA, DMA((15,)), DMA((15,)),
         DMA((15,)), DMA((15,)), DMA((15,)), DMA((15,)), DMA((15,)), DMA((15,)),
-        DMA((7,)), DMA((7,)), DMA, DMA, DMA((15,)), DMA((15,)),
+        DMA((15,)), DMA((15,)), DMA, DMA, DMA((15,)), DMA((15,)), DMA((7,)), DMA((7,)),
     ]
-    whole = jax.ShapeDtypeStruct((2, 12, 56, D), F32)
+    whole = jax.ShapeDtypeStruct((2, 9, 48, D), F32)
     edge = jax.ShapeDtypeStruct((2, 3, 48, D), F32)
     side = jax.ShapeDtypeStruct((2, 12, 8, D), F32)
     return pl.pallas_call(
         main_kernel,
         out_shape=[
             whole, whole, edge, edge, side, side,
-            jax.ShapeDtypeStruct((8, 2, 5, 16, 128), F32),
+            jax.ShapeDtypeStruct((16, 2, 40, 128), F32),
             jax.ShapeDtypeStruct((16, 16, 128), F32), jax.ShapeDtypeStruct((16, 16, 128), F32),
         ],
         in_specs=[anywhere] * 2 + [vm] * 4,
-        out_specs=[vm] * 9,
+        out_specs=[anywhere] * 2 + [vm] * 7,
         scratch_shapes=scratch,
         compiler_params=pltpu.CompilerParams(
             collective_id=0, has_side_effects=True, vmem_limit_bytes=60 * 1024 * 1024),
@@ -536,14 +579,14 @@
 ):
     for ext, rows, cols, out in ((ext_b, rows_b, cols_b, branch), (ext_g, rows_g, cols_g, grads)):
         out[:, 0:3] = rows[...]
-        out[:, 3:12] = ext[:, 0:9, 0:48, :]
+        out[:, 3:12] = ext[...]
         there = lax.broadcasted_iota(jnp.int32, (2, 12, 8, D), 2) < 6
         out[:, :, 0:8, :] = jnp.where(there, cols[...], out[:, :, 0:8, :])
     scale = 1.0 / math.sqrt(LATS * LONS * WINDOWS * TOK)
     for i in range(24):
         for j in range(6):
-            q, s = divmod(i * 6 + j, 9)
-            full[i * 8:i * 8 + 8, j * 128:(j + 1) * 128] = total[q // 2, q % 2, s // 2, s % 2 * 8:s % 2 * 8 + 8, :] * scale
+            q, s = divmod(i * 6 + j, 5)
+            full[i * 8:i * 8 + 8, j * 128:(j + 1) * 128] = total[q // 2, q % 2, s * 8:s * 8 + 8, :] * scale
     raw = full[:, :3 * D]
     summed = jnp.sum(raw * wqkv_ref[...], axis=1, keepdims=True)
     gain_out[...] = jnp.broadcast_to(summed, (D, 128)).T[:1]

time: 97 us -> 97.3 us (level)
  no operation moved by 1% of the time
where the time goes in v1:
time: 97.3 us; the launch traced here: 97.2 us
  Pallas kernels  96.5 us (99%)
    pallas_call x1, Pallas kernels, main(): pl.pallas_call(main_kernel, out_shape=[whole, whole, edge, edge, side, si...  92.2 us
    pallas_call x1, Pallas kernels, finish(): pl.pallas_call(finish_kernel, out_shape=[whole, whole, jax.ShapeDtypeStru...  4.28 us

profile of v1, /device:TPU:1, one launch (start us, length us, event | category | flops | bytes accessed | tf_op | source)
XLA Modules:
  0.0 97.2 jit_solution(6780819985772836389)
XLA Ops:
  0.6 92.2 %shard_map.109 = (f32[2,9,48,192]{3,2,1,0:T(8,128)}, f32[2,9,48,192]{3,2,1,0:T(8,128)}, f32[2,3,48,192]{3,2,1,0:T(8,128)}, f32[2,3,48,192]{3,2,1,0:T(8,128)}, f3...) custom-call(f32[2,12,48,192]{3,2,1,0:T(8,128)} %f_ref.1, ...), custom_call_target="tpu_custom_call" | custom-call | tf_op jit(solution)/shard_map/pallas_call | solution.py:561
  92.9 4.3 %shard_map.110 = (f32[2,12,48,192]{3,2,1,0:T(8,128)}, f32[2,12,48,192]{3,2,1,0:T(8,128)}, f32[1,192]{1,0:T(1,128)}, f32[192,576]{1,0:T(8,128)}, f32[192,192]{1,0:T(8,128)}, /*index=5*/f32[6,2,3312]{2,1,0:T(2,128)}) custom-call(f32[2,9,48,192]{3,2,1,0:T(8,128)} %get-tuple-element.21.ext_b, f32[2,9,48,192]{3,2,1,0:T(8,128)} %get-tuple-element.22.ext_g, ...), custom_call_target="tpu_custom_call" | custom-call | tf_op jit(solution)/shard_map/pallas_call | solution.py:617

commit v2 on v1

--- a/solution.py
+++ b/solution.py
@@ -105,18 +105,6 @@
     greet((down, lon))
     greet((up, right))
     greet((down, left))
-    pl.semaphore_wait(barrier, 33)
-    halos_in = []
-    for i, (src, dst) in enumerate(((f_ref, ext_f), (g_ref, ext_g))):
-        pieces = (
-            (src.at[:, pl.ds(3, 9), pl.ds(0, 8)], dst.at[:, pl.ds(0, 9), pl.ds(48, 8)], (lat, left)),
-            (src.at[:, pl.ds(0, 3), pl.ds(0, 8)], dst.at[:, pl.ds(9, 3), pl.ds(48, 8)], (down, left)),
-            (src.at[:, pl.ds(0, 3)], dst.at[:, pl.ds(9, 3), pl.ds(0, 48)], (down, lon)),
-        )
-        for j, (a, b, target) in enumerate(pieces):
-            copy = remote(a, b, in_send.at[i * 3 + j], in_recv.at[i * 3 + j], target)
-            copy.start()
-            halos_in.append(copy)
 
     factor = HEAD ** (-0.5)
     gain = gain_ref[...]
@@ -219,6 +207,19 @@
         dh, dl = split(mm3(split(ups[rows, :]), wo, NT))
         do_hi[rows, :] = dh
         do_lo[rows, :] = dl
+
+    pl.semaphore_wait(barrier, 33)
+    halos_in = []
+    for i, (src, dst) in enumerate(((f_ref, ext_f), (g_ref, ext_g))):
+        pieces = (
+            (src.at[:, pl.ds(3, 9), pl.ds(0, 8)], dst.at[:, pl.ds(0, 9), pl.ds(48, 8)], (lat, left)),
+            (src.at[:, pl.ds(0, 3), pl.ds(0, 8)], dst.at[:, pl.ds(9, 3), pl.ds(48, 8)], (down, left)),
+            (src.at[:, pl.ds(0, 3)], dst.at[:, pl.ds(9, 3), pl.ds(0, 48)], (down, lon)),
+        )
+        for j, (a, b, target) in enumerate(pieces):
+            copy = remote(a, b, in_send.at[i * 3 + j], in_recv.at[i * 3 + j], target)
+            copy.start()
+            halos_in.append(copy)
 
     for copy in local:
         copy.wait()

time: 97.3 us -> 97.1 us (level)
  no operation moved by 1% of the time
where the time goes in v2:
time: 97.1 us; the launch traced here: 97 us
  Pallas kernels  96.4 us (99%)
    pallas_call x1, Pallas kernels, main(): pl.pallas_call(main_kernel, out_shape=[whole, whole, edge, edge, side, si...  92.1 us
    pallas_call x1, Pallas kernels, finish(): pl.pallas_call(finish_kernel, out_shape=[whole, whole, jax.ShapeDtypeStru...  4.28 us

profile of v2, /device:TPU:1, one launch (start us, length us, event | category | flops | bytes accessed | tf_op | source)
XLA Modules:
  0.0 97.0 jit_solution(9092566649064363662)
XLA Ops:
  0.6 92.1 %shard_map.109 = (f32[2,9,48,192]{3,2,1,0:T(8,128)}, f32[2,9,48,192]{3,2,1,0:T(8,128)}, f32[2,3,48,192]{3,2,1,0:T(8,128)}, f32[2,3,48,192]{3,2,1,0:T(8,128)}, f3...) custom-call(f32[2,12,48,192]{3,2,1,0:T(8,128)} %f_ref.1, ...), custom_call_target="tpu_custom_call" | custom-call | tf_op jit(solution)/shard_map/pallas_call | solution.py:562
  92.7 4.3 %shard_map.110 = (f32[2,12,48,192]{3,2,1,0:T(8,128)}, f32[2,12,48,192]{3,2,1,0:T(8,128)}, f32[1,192]{1,0:T(1,128)}, f32[192,576]{1,0:T(8,128)}, f32[192,192]{1,0:T(8,128)}, /*index=5*/f32[6,2,3312]{2,1,0:T(2,128)}) custom-call(f32[2,9,48,192]{3,2,1,0:T(8,128)} %get-tuple-element.21.ext_b, f32[2,9,48,192]{3,2,1,0:T(8,128)} %get-tuple-element.22.ext_g, ...), custom_call_target="tpu_custom_call" | custom-call | tf_op jit(solution)/shard_map/pallas_call | solution.py:618
